TPU v7x, 32 devices: a whole 2x2x4 slice. The times are simulated.
32 devices in a mesh: dp: 4 (over y, x), tensor: 8 (over z, core).
Axes of the slice: x: 2, y: 2, z: 4, core: 2. Of those that a mesh axis runs over, the one named last changes fastest.
Arguments:
- tokens: bfloat16 [128, 8192], P(('dp', 'tensor')), may hold values from -16 to 16
- gate_weight: bfloat16 [8192, 16384], P('dp', 'tensor'), may hold values from -0.0625 to 0.0625
- up_weight: bfloat16 [8192, 16384], P('dp', 'tensor'), may hold values from -0.0625 to 0.0625
- cotangent: bfloat16 [128, 16384], P('dp', 'tensor'), may hold values from -13 to 13
Outputs:
- hidden: bfloat16 [128, 16384], P('dp', 'tensor')
- grad_tokens: bfloat16 [128, 8192], P(('dp', 'tensor'))
- grad_gate: bfloat16 [8192, 16384], P('dp', 'tensor')
- grad_up: bfloat16 [8192, 16384], P('dp', 'tensor')
- token_descale: float32 [], replicated
- grad_descale: float32 [], replicated
All inputs are finite; a program needn't handle non-finite values. Where the computation divides by a largest or mean magnitude, that divisor is 1e-20 or more.
Results may differ from a plain program's by a relative error of at most 0.02.
Values may be sent and summed in bfloat16 or wider, within the bound.
A program may use at most 256 MiB of HBM per device.

v0:
```python
import jax
import jax.numpy as jnp
from jax import lax
from jax.sharding import PartitionSpec as P

FP_MAX = 448.0
EPSILON = 1e-06


def settle(value_entries):
    return lax.optimization_barrier(value_entries.astype(jnp.bfloat16)).astype(jnp.float32)


def local(tokens, gate_weight, up_weight, cotangent):
    replicas = lax.axis_size("dp")
    tokens_per_shard, model_width = tokens.shape
    slice_width = model_width // replicas
    units = gate_weight.shape[1]
    token_peak = lax.pmax(jnp.max(jnp.abs(tokens)).astype(jnp.float32), ("dp", "tensor"))
    moving = (tokens.astype(jnp.float32) * (FP_MAX / (token_peak + EPSILON))).astype(jnp.bfloat16)
    gathered = lax.all_gather(moving, "tensor", axis=0, tiled=True)
    spread = lax.all_to_all(
        gathered.reshape(1, gathered.shape[0], model_width),
        "dp",
        split_axis=2,
        concat_axis=0,
        tiled=True,
    )
    token_descale = (token_peak + EPSILON) / FP_MAX
    tokens_per_replica = spread.shape[1]
    weight_matrices = jnp.concatenate([gate_weight, up_weight], axis=1)
    flat_rows = spread.reshape(replicas * tokens_per_replica, slice_width)
    block_of_rows = flat_rows
    paired = (
        lax.psum_scatter(
            jnp.dot(block_of_rows, weight_matrices, preferred_element_type=jnp.float32).astype(
                jnp.bfloat16
            ),
            "dp",
            scatter_dimension=0,
            tiled=True,
        ).astype(jnp.float32)
        * token_descale
    )
    gate_act = paired[:, :units]
    up_act = paired[:, units:]
    sigmoid_gate = jax.nn.sigmoid(gate_act)
    silu_gate = gate_act * sigmoid_gate
    hidden = (silu_gate * up_act).astype(jnp.bfloat16)
    cot_values = cotangent.astype(jnp.float32)
    gate_gradient = cot_values * up_act * sigmoid_gate * (1.0 + gate_act * (1.0 - sigmoid_gate))
    d_up = cot_values * silu_gate
    grad_pair = jnp.concatenate([gate_gradient, d_up], axis=1)
    grad_peak = lax.pmax(jnp.max(jnp.abs(grad_pair)), ("dp", "tensor"))
    grad_descale = (grad_peak + EPSILON) / FP_MAX
    grad_quant = (grad_pair * (FP_MAX / (grad_peak + EPSILON))).astype(jnp.bfloat16)
    all_grads = lax.all_gather(
        grad_quant.reshape(tokens_per_replica, 1, 2 * units), "dp", axis=1, tiled=True
    )
    both_descale = token_descale * grad_descale
    contract = (((0,), (0,)), ((), ()))

    def add_replica(replica, grad_total):
        token_rows = lax.dynamic_index_in_dim(spread, replica, 0, keepdims=False)
        grad_cols = lax.dynamic_index_in_dim(all_grads, replica, 1, keepdims=False)
        matrix_product = lax.dot_general(
            token_rows, grad_cols, contract, preferred_element_type=jnp.float32
        )
        return grad_total + settle(matrix_product * both_descale)

    grad_total = lax.fori_loop(
        0, replicas, add_replica, jnp.zeros((slice_width, 2 * units), jnp.float32)
    )
    grad_gate = grad_total[:, :units].astype(jnp.bfloat16)
    grad_up = grad_total[:, units:].astype(jnp.bfloat16)
    block_of_rows = all_grads
    matrix_product = jnp.einsum(
        "zmc,vc->zmv", block_of_rows, weight_matrices, preferred_element_type=jnp.float32
    )
    back_rows = lax.psum_scatter(
        (matrix_product * grad_descale).astype(jnp.bfloat16),
        "tensor",
        scatter_dimension=0,
        tiled=True,
    )
    own_rows = lax.all_to_all(back_rows, "dp", split_axis=1, concat_axis=2, tiled=True)
    grad_tokens = own_rows.reshape(tokens_per_shard, model_width)
    return (hidden, grad_tokens, grad_gate, grad_up, token_descale, grad_descale)


def solution(mesh):
    return jax.shard_map(
        local,
        mesh=mesh,
        in_specs=(
            P(("dp", "tensor"), None),
            P("dp", "tensor"),
            P("dp", "tensor"),
            P("dp", "tensor"),
        ),
        out_specs=(
            P("dp", "tensor"),
            P(("dp", "tensor"), None),
            P("dp", "tensor"),
            P("dp", "tensor"),
            P(),
            P(),
        ),
        check_vma=False,
    )
```

profile of v0, /device:TPU:0, one launch (start us, length us, event | category | flops | bytes accessed | tf_op | source)
XLA Modules:
  0.0 456.5 jit_solution(7746790422312258824)
XLA Ops:
  7.2 1.5 abs_reduce_fusion
  8.7 42.2 %pmax.14 = f32[]{:T(128)} all-reduce(bf16[]{:T(256)} %abs_reduce_fusion), channel_id=1, replica_groups=mesh['dp'=4,'tensor'=8] {'dp','tensor'}, use_global_device_ids=true, to_apply=%region_1.0 | all-reduce | flops 1 | bytes 6 | tf_op jit(solution)/shard_map/pmax | solution.py:19
  51.6 0.9 fusion.18
  52.5 15.0 %all-gather = bf16[8,4,8192]{2,1,0:T(4,128)(2,1)S(1)} all-gather(bf16[1,4,8192]{2,1,0:T(4,128)(2,1)S(1)} %fusion.18), channel_id=1, replica_groups=mesh['dp'=4,'tensor'=8] {'tensor'}, dimensions={0}, use_global_device_ids=true | all-gather | bytes 589824 | tf_op jit(solution)/shard_map/all_gather | solution.py:21
  67.5 0.1 reshape.59
  67.6 6.7 %copy.14 = bf16[1,32,8192]{1,0,2:T(2,128)(2,1)} copy(bf16[1,32,8192]{2,1,0:T(8,128)(2,1)S(1)} %reshape.59) | data formatting | bytes 1048576 | tf_op jit(solution)/shard_map/reshape | solution.py:23
  74.3 0.5 broadcast.23
  74.8 45.2 %reduce = bf16[8192,32]{1,0:T(8,128)(2,1)S(1)} reduce(bf16[8192,1,32]{2,1,0:T(2,128)(2,1)} %bitcast.32, bf16[]{:T(256)} %broadcast.23), dimensions={1}, to_apply=%bitcast.23.reduce_sub_computation | reduce | bytes 1048578
  120.0 2.9 reshape.69
  122.9 3.8 all-to-all-start
  126.8 0.0 reduce-scatter.3.cloned.1.call-start
  126.8 8.3 %constant_dynamic-update-slice_fusion.1 = bf16[2048,4096]{1,0:T(8,128)(2,1)} fusion(bf16[2048,2048]{1,0:T(8,128)(2,1)} %param.7), kind=kLoop, calls=%fused_computation.28 | loop fusion | bytes 16777216
  135.0 8.2 %constant_dynamic-update-slice_fusion = bf16[2048,4096]{1,0:T(8,128)(2,1)} fusion(bf16[2048,4096]{1,0:T(8,128)(2,1)} %constant_dynamic-update-slice_fusion.1, bf16[2048,2048]{1,0:T(8,128)(2,1)} %param.8), kind=kLoop, calls=%fused_computation.27 | loop fusion | bytes 16777216 | tf_op jit(solution)/shard_map/concatenate | solution.py:31
  143.3 0.0 all-to-all-done
  143.3 3.3 reshape.70
  146.5 8.0 %copy.15 = bf16[1,32,8192]{2,1,0:T(8,128)(2,1)S(1)} copy(bf16[1,32,8192]{1,0,2:T(2,128)(2,1)} %bitcast.33) | data formatting | bytes 1048576 | tf_op jit(solution)/shard_map/all_to_all | solution.py:22
  154.5 0.4 all_to_all.21
  154.9 0.3 copy.16
  155.2 9.1 %convolution_convert_fusion = bf16[128,4096]{1,0:T(8,128)(2,1)} fusion(bf16[128,2048]{1,0:T(8,128)(2,1)S(1)} %bitcast.36, bf16[2048,4096]{1,0:T(8,128)(2,1)} %constant_dynamic-update-slice_fusion), kind=kOutput, calls=%fused_computation.9 | convolution fusion | flops 2148007936 | bytes 18350080 | tf_op jit(solution)/shard_map/dot_general | solution.py:36
  164.3 0.0 reduce-scatter.3.cloned.1.call-update
  164.4 0.0 all-gather.3.cloned.1.call-start
  164.4 28.1 %reduce-scatter.3.cloned.1.call-done = bf16[32,4096]{1,0:T(8,128)(2,1)} async-done(((bf16[128,4096]{1,0:T(8,128)(2,1)}), bf16[32,4096]{1,0:T(8,128)(2,1)}) %reduce-scatter.3.cloned.1.call-update) | async-done | bytes 262160 | tf_op jit(solution)/shard_map/reduce_scatter | solution.py:35
  192.5 1.0 convert_multiply_fusion
  193.5 0.8 fusion.16
  194.3 0.6 fusion.14
  194.9 39.5 %pmax.15 = f32[]{:T(128)} all-reduce(f32[]{:T(128)} %fusion.14), channel_id=1, replica_groups=mesh['dp'=4,'tensor'=8] {'dp','tensor'}, use_global_device_ids=true, to_apply=%region_4.0 | all-reduce | flops 1 | bytes 8 | tf_op jit(solution)/shard_map/pmax | solution.py:54
  235.1 0.7 fusion.13
  235.9 0.0 all-gather.3.cloned.1.call-update
  235.9 0.3 all-reduce.3.cloned.1.call-start
  236.2 0.6 dynamic-slice
  237.4 0.3 copy.17
  237.7 25.9 %all-gather.3.cloned.1.call-done = bf16[32,4,4096]{2,0,1:T(8,128)(2,1)} async-done(((bf16[32,1,4096]{2,0,1:T(8,128)(2,1)}), bf16[32,4,4096]{2,0,1:T(8,128)(2,1)}) %all-gather.3.cloned.1.call-update) | async-done | bytes 1048592 | tf_op jit(solution)/shard_map/all_gather | solution.py:57
  263.6 12.6 %fusion.10 = bf16[32,4,2048]{2,0,1:T(8,128)(2,1)} fusion(bf16[32,4,4096]{2,0,1:T(8,128)(2,1)} %all-gather.3.cloned.1.call-done, bf16[2048,4096]{1,0:T(8,128)(2,1)} %constant_dynamic-update-slice_fusion, f32[]{:T(128)} %div.19), kind=kOutput, calls=%fused_computation.11 | convolution fusion | flops 2148007936 | bytes 18350084 | tf_op jit(solution)/shard_map/zmc,vc->zmv/dot_general | solution.py:77
  276.1 0.0 all-reduce.3.cloned.1.call-update
  276.2 136.7 %while.14 = (s32[]{:T(128)}, f32[2048,4096]{1,0:T(8,128)}, bf16[4,32,2048]{2,1,0:T(8,128)(2,1)S(1)}, bf16[32,4,4096]{2,0,1:T(8,128)(2,1)}, f32[]{:T(128)}, /*index=5*/s32[]{:T(128)}, s32[]{:T(128)}) while((s32[]{:T(128)}, f32[2048,4096]{1,0:T(8,128)}, bf16[4,32,2048]{2,1,0:T(8,128)(2,1)S(1)}, bf16[32,4,4096]{2,0,1:T(8,128)(2,1)}, ...), condition=%wide.region_7.8_spmd.clone, body=%wide.region_6.7_spmd.clone.sunk | while | flops 578813952 | bytes 101058144 | solution.py:71
  276.2 9.1 %multiply_convert_fusion.4 = bf16[2048,4096]{1,0:T(8,128)(2,1)} fusion(f32[]{:T(128)} %get-tuple-element.203, bf16[32,4,4096]{2,0,1:T(8,128)(2,1)} %get-tuple-element.202, s32[]{:T(128)S(6)} %copy.24, bf16[4,32,2048]{2,1,0:T(8,128)(2,1)S(1)} %get-tuple-element.201), kind=kOutput, calls=%fused_computation.1.clone.1 | convolution fusion | flops 553648128 | bytes 17171968 | tf_op jit(solution)/shard_map/while/body/eval_jaxpr/dot_general | solution.py:66
  285.2 19.1 %select_add_fusion.2 = f32[2048,4096]{1,0:T(8,128)} fusion(f32[2048,4096]{1,0:T(8,128)} %get-tuple-element.193, bf16[2048,4096]{1,0:T(8,128)(2,1)} %multiply_convert_fusion.4, pred[]{:T(512)S(6)} %compare.3), kind=kLoop, calls=%fused_computation.clone.1 | loop fusion | flops 25165824 | bytes 83886080 | tf_op jit(solution)/shard_map/while/body/eval_jaxpr/add | solution.py:69
  304.3 9.0 %multiply_convert_fusion.4 = bf16[2048,4096]{1,0:T(8,128)(2,1)} fusion(f32[]{:T(128)} %get-tuple-element.203, bf16[32,4,4096]{2,0,1:T(8,128)(2,1)} %get-tuple-element.202, s32[]{:T(128)S(6)} %copy.24, bf16[4,32,2048]{2,1,0:T(8,128)(2,1)S(1)} %get-tuple-element.201), kind=kOutput, calls=%fused_computation.1.clone.1 | convolution fusion | flops 553648128 | bytes 17171968 | tf_op jit(solution)/shard_map/while/body/eval_jaxpr/dot_general | solution.py:66
  313.4 27.3 %select_add_fusion.2 = f32[2048,4096]{1,0:T(8,128)} fusion(f32[2048,4096]{1,0:T(8,128)} %get-tuple-element.193, bf16[2048,4096]{1,0:T(8,128)(2,1)} %multiply_convert_fusion.4, pred[]{:T(512)S(6)} %compare.3), kind=kLoop, calls=%fused_computation.clone.1 | loop fusion | flops 25165824 | bytes 83886080 | tf_op jit(solution)/shard_map/while/body/eval_jaxpr/add | solution.py:69
  340.6 9.0 %multiply_convert_fusion.4 = bf16[2048,4096]{1,0:T(8,128)(2,1)} fusion(f32[]{:T(128)} %get-tuple-element.203, bf16[32,4,4096]{2,0,1:T(8,128)(2,1)} %get-tuple-element.202, s32[]{:T(128)S(6)} %copy.24, bf16[4,32,2048]{2,1,0:T(8,128)(2,1)S(1)} %get-tuple-element.201), kind=kOutput, calls=%fused_computation.1.clone.1 | convolution fusion | flops 553648128 | bytes 17171968 | tf_op jit(solution)/shard_map/while/body/eval_jaxpr/dot_general | solution.py:66
  349.7 27.1 %select_add_fusion.2 = f32[2048,4096]{1,0:T(8,128)} fusion(f32[2048,4096]{1,0:T(8,128)} %get-tuple-element.193, bf16[2048,4096]{1,0:T(8,128)(2,1)} %multiply_convert_fusion.4, pred[]{:T(512)S(6)} %compare.3), kind=kLoop, calls=%fused_computation.clone.1 | loop fusion | flops 25165824 | bytes 83886080 | tf_op jit(solution)/shard_map/while/body/eval_jaxpr/add | solution.py:69
  376.7 9.0 %multiply_convert_fusion.4 = bf16[2048,4096]{1,0:T(8,128)(2,1)} fusion(f32[]{:T(128)} %get-tuple-element.203, bf16[32,4,4096]{2,0,1:T(8,128)(2,1)} %get-tuple-element.202, s32[]{:T(128)S(6)} %copy.24, bf16[4,32,2048]{2,1,0:T(8,128)(2,1)S(1)} %get-tuple-element.201), kind=kOutput, calls=%fused_computation.1.clone.1 | convolution fusion | flops 553648128 | bytes 17171968 | tf_op jit(solution)/shard_map/while/body/eval_jaxpr/dot_general | solution.py:66
  385.8 27.1 %select_add_fusion.2 = f32[2048,4096]{1,0:T(8,128)} fusion(f32[2048,4096]{1,0:T(8,128)} %get-tuple-element.193, bf16[2048,4096]{1,0:T(8,128)(2,1)} %multiply_convert_fusion.4, pred[]{:T(512)S(6)} %compare.3), kind=kLoop, calls=%fused_computation.clone.1 | loop fusion | flops 25165824 | bytes 83886080 | tf_op jit(solution)/shard_map/while/body/eval_jaxpr/add | solution.py:69
  412.9 17.4 %convert.4 = bf16[2048,4096]{1,0:T(8,128)(2,1)} convert(f32[2048,4096]{1,0:T(8,128)} %get-tuple-element.100) | non-fusion elementwise | flops 8388608 | bytes 50331648 | tf_op jit(solution)/shard_map/convert.1
  430.2 1.6 constant_dynamic-slice_fusion
  431.8 3.3 all-to-all-start.1
  435.1 12.0 %fusion.19 = (bf16[2048,2048]{1,0:T(8,128)(2,1)}, bf16[2048,2048]{1,0:T(8,128)(2,1)}) fusion(bf16[2048,4096]{1,0:T(8,128)(2,1)} %convert.4), kind=kLoop, calls=%fused_computation.30 | loop fusion | bytes 33554432 | tf_op jit(solution)/shard_map/slice | solution.py:75
  447.0 0.6 copy.29
  (7 shorter events, 0.0 us)
Async XLA Ops:
  122.9 20.3 %all-to-all-start = ((bf16[4,2,32768]{2,1,0:T(2,128)(2,1)}), bf16[4,2,32768]{2,1,0:T(2,128)(2,1)S(1)}, u32[]{:S(2)}, u32[]{:S(2)}) async-start(bf16[4,2,32768]{2,1,0:T(2,128)(2,1)} %reshape.69), calls=%async_computation | async-start | bytes 1048576 | tf_op jit(solution)/shard_map/all_to_all | solution.py:22
  126.8 65.7 %reduce-scatter.3.cloned.1.call-start = ((), (), s32[]{:S(2)}) async-start(), calls=%async_computation.3 | async-start | bytes 1310720 | tf_op jit(solution)/shard_map/reduce_scatter | solution.py:35
  146.5 46.9 %copy-start = (bf16[32,2048]{1,0:T(8,128)(2,1)S(1)}, bf16[32,2048]{1,0:T(8,128)(2,1)}, u32[]{:S(2)}) copy-start(bf16[32,2048]{1,0:T(8,128)(2,1)} %param.9) | copy-start | bytes 393220
  146.5 89.6 %copy-start.1 = (u32[32]{0:T(128)S(1)}, u32[32]{0:T(128)}, u32[]{:S(2)}) copy-start(u32[32]{0:T(128)} %constant.50) | copy-start | bytes 388
  164.4 99.2 %all-gather.3.cloned.1.call-start = ((), (), s32[]{:S(2)}) async-start(), calls=%async_computation.4 | async-start | bytes 1310720 | tf_op jit(solution)/shard_map/all_gather | solution.py:57
  235.9 194.3 %all-reduce.3.cloned.1.call-start = ((), (), s32[]{:S(2)}) async-start(), calls=%async_computation.5 | async-start | bytes 1048576
  431.8 15.3 %all-to-all-start.1 = ((bf16[4,4,2048]{2,0,1:T(4,128)(2,1)}), bf16[4,4,2048]{2,0,1:T(4,128)(2,1)S(1)}, u32[]{:S(2)}, u32[]{:S(2)}) async-start(bf16[4,4,2048]{2,0,1:T(4,128)(2,1)} %constant_dynamic-slice_fusion), calls=%async_computation.2 | async-start | bytes 131072 | tf_op jit(solution)/shard_map/all_to_all | solution.py:86
Sparse Core Ops, SparseCore 0:
  164.5 27.9 reduce-scatter.2
  236.0 27.5 all-gather.2
  276.3 56.1 all-reduce.2
where the time goes:
time: 458 us; the launch traced here: 456 us
  other arithmetic  169 us (37%)
  blocking collectives  96.7 us (21%)
  matrix products  57.8 us (13%)
  waiting for transfers between devices  54 us (12%)
  local copies, waits for them, and re-layouts  53.7 us (12%)
  between operations  18.1 us (4%)
  starting transfers between devices  7.41 us (2%)
    add x4, other arithmetic, add_replica(): return grad_total + settle(matrix_product * both_descale)  101 us
    unnamed x3, other arithmetic  46.1 us
    pmax x1, blocking collectives, local(): lax.pmax(jnp.max(jnp.abs(tokens)).astype(jnp.float32), ('dp', 'tensor'))  42.2 us
    pmax x1, blocking collectives, local(): grad_peak = lax.pmax(jnp.max(jnp.abs(grad_pair)), ('dp', 'tensor'))  39.5 us
    dot_general x4, matrix products, add_replica(): lax.dot_general(token_rows, grad_cols, contract, preferred_element_type=j...  36.1 us
    reduce_scatter x1, waiting for transfers between devices, local(): lax.psum_scatter(jnp.dot(block_of_rows, weight_matrices, preferred_elemen...  28.1 us
    all_gather x1, waiting for transfers between devices, local(): lax.all_gather(grad_quant.reshape(tokens_per_replica, 1, 2 * units), 'dp'...  25.9 us
    unnamed x12, local copies, waits for them, and re-layouts  18 us
  transfers between devices with their start and end apart: 5, of which 2 were waited for; matrix products, arithmetic and copies ran while one was open for 40% of the time, Pallas kernels for 0%

commit v1 on v0

v1 whole, which is shorter than its diff:
```python
import functools

import jax
import jax.numpy as jnp
import numpy as np
from jax import lax
from jax.experimental import pallas as pl
from jax.experimental.pallas import tpu as pltpu
from jax.sharding import PartitionSpec as P

FP_MAX = 448.0
EPSILON = 1e-06
CHUNKS = 4
MESH = pl.DeviceIdType.MESH
F32 = jnp.float32
BF16 = jnp.bfloat16


def remote(src, dst, send, recv, device):
    return pltpu.make_async_remote_copy(
        src_ref=src, dst_ref=dst, send_sem=send, recv_sem=recv, device_id=device, device_id_type=MESH
    )


def lane_peak(values, rows):
    peak = None
    for at in range(0, values.shape[0], rows):
        for lane in range(0, values.shape[1], 128):
            piece = values[at : at + rows, lane : lane + 128]
            peak = piece if peak is None else jnp.maximum(peak, piece)
    return peak


def exchange(
    nd, nt,
    tok, gate_hbm, up_hbm, cot, perm,
    hid, x, g, gtok, peaks,
    wg, wu, blocks, wide, xt, part, inbox, dx, dxp, pair_in, line_out, line_in, back,
    stats, st_dp, st_pair, st_line,
    w_sem, a_s, a_r, b_s, b_r, f_s, f_r, p_s, p_r, rs_s, rs_r, ag_s, ag_r,
    l_s, l_r, o_s, o_r, sd_s, sd_r, sp_s, sp_r, sl_s, sl_r,
):
    d = lax.axis_index("dp")
    t = lax.axis_index("tensor")
    core = lax.rem(t, 2)
    z = t // 2
    nz = nt // 2
    sib = t + 1 - 2 * core
    tl = tok.shape[0]
    s, units = gate_hbm.shape
    r = cot.shape[0]
    total = nd * r
    rows = nd * tl
    uc = units // CHUNKS
    tile = min(256, s)
    dp_to = [lax.rem(d + k, nd) for k in range(nd)]
    z_to = [lax.rem(z + k, nz) for k in range(nz)]
    z_from = [lax.rem(z + nz - k, nz) for k in range(nz)]

    def weight_copies(c):
        cols = pl.ds(pl.multiple_of(c * uc, 128), uc)
        return (
            pltpu.make_async_copy(gate_hbm.at[:, cols], wg.at[:, cols], w_sem.at[0, c]),
            pltpu.make_async_copy(up_hbm.at[:, cols], wu.at[:, cols], w_sem.at[1, c]),
        )

    for c in range(CHUNKS):
        for copy in weight_copies(c):
            copy.start()

    barrier = pltpu.get_barrier_semaphore()
    for k in range(1, nd):
        pl.semaphore_signal(barrier, inc=1, device_id=(dp_to[k], t), device_id_type=MESH)
    for k in range(1, nz):
        pl.semaphore_signal(barrier, inc=1, device_id=(d, 2 * z_to[k] + core), device_id_type=MESH)
    pl.semaphore_signal(barrier, inc=1, device_id=(d, sib), device_id_type=MESH)
    pl.semaphore_wait(barrier, nd + nz - 1)

    def feature_cols(i):
        return pl.ds(pl.multiple_of(i * s, 128), s)

    sends = []
    first = []
    for k in range(1, nd):
        copy = remote(tok.at[:, feature_cols(dp_to[k])], blocks.at[d], a_s.at[k], a_r.at[k], (dp_to[k], t))
        copy.start()
        first.append(copy)
    blocks[d] = tok[:, feature_cols(d)]
    token_peak = lane_peak(jnp.abs(tok[...].astype(F32)), tl)
    stats[0] = jnp.broadcast_to(jnp.max(token_peak, axis=0, keepdims=True), (8, 128))
    for copy in first:
        copy.wait_recv()
    sends += first
    for i in range(nd):
        wide[i * tl : (i + 1) * tl, :] = blocks[i].astype(F32)
    xt[t] = wide[...].astype(BF16)

    along = [
        remote(xt.at[t], xt.at[t], b_s.at[k], b_r.at[k], (d, 2 * z_to[k] + core)) for k in range(1, nz)
    ]
    for copy in along:
        copy.start()
    across = [remote(xt.at[t], xt.at[t], f_s.at[0], f_r.at[0], (d, sib))]
    across[0].start()
    for k in range(1, nz):
        along[k - 1].wait_recv()
        slot = 2 * z_from[k] + core
        copy = remote(xt.at[slot], xt.at[slot], f_s.at[k], f_r.at[k], (d, sib))
        copy.start()
        across.append(copy)
    for copy in across:
        copy.wait_recv()
    sends += along + across

    @pl.loop(0, s // tile)
    def _(j):
        cols = pl.ds(pl.multiple_of(j * tile, 128), tile)
        lined = xt[:, :, cols].reshape(total, tile)
        x[:, cols] = jnp.dot(perm[0], lined, preferred_element_type=F32).astype(BF16)
        dx[:, cols] = jnp.zeros((total, tile), F32)

    def partial_copy(c, k):
        return remote(part.at[c, dp_to[k]], inbox.at[c, k - 1], rs_s.at[c, k], rs_r.at[c, k], (dp_to[k], t))

    wide_tile = min(256, uc)

    @pl.loop(0, CHUNKS)
    def _(c):
        for copy in weight_copies(c):
            copy.wait()
        for side, w in ((0, wg), (1, wu)):
            for at in range(0, uc, wide_tile):
                cols = pl.ds(pl.multiple_of(c * uc + at, 128), wide_tile)
                product = jnp.dot(x[...], w[:, cols], preferred_element_type=F32)
                part[c, :, side, :, at : at + wide_tile] = product.astype(BF16).reshape(nd, r, wide_tile)
        for k in range(1, nd):
            partial_copy(c, k).start()

    def grad_copy(c, k):
        return remote(g.at[c, d], g.at[c, d], ag_s.at[c, k], ag_r.at[c, k], (dp_to[k], t))

    def activate(c, peak):
        for k in range(1, nd):
            partial_copy(c, k).wait_recv()
        cols = pl.ds(pl.multiple_of(c * uc, 128), uc)
        gate = part[c, d, 0].astype(F32)
        up = part[c, d, 1].astype(F32)
        for k in range(1, nd):
            gate = gate + inbox[c, k - 1, 0].astype(F32)
            up = up + inbox[c, k - 1, 1].astype(F32)
        sig = jax.nn.sigmoid(gate)
        silu = gate * sig
        hid[:, cols] = (silu * up).astype(BF16)
        cotangent = cot[:, cols].astype(F32)
        d_gate = cotangent * up * sig * (1.0 + gate * (1.0 - sig))
        d_up = cotangent * silu
        g[c, d, 0] = d_gate.astype(BF16)
        g[c, d, 1] = d_up.astype(BF16)
        for k in range(1, nd):
            grad_copy(c, k).start()
        return jnp.maximum(peak, lane_peak(jnp.maximum(jnp.abs(d_gate), jnp.abs(d_up)), 8))

    stats[1] = lax.fori_loop(0, CHUNKS, activate, jnp.zeros((8, 128), F32))
    peak_dp = [remote(stats, st_dp.at[k - 1], sd_s.at[k], sd_r.at[k], (dp_to[k], t)) for k in range(1, nd)]
    for copy in peak_dp:
        copy.start()

    contract = (((1,), (1,)), ((), ()))

    @pl.loop(0, CHUNKS)
    def _(c):
        for k in range(1, nd):
            grad_copy(c, k).wait_recv()
        units_here = pl.ds(pl.multiple_of(c * uc, 128), uc)

        @pl.loop(0, s // tile)
        def _(j):
            cols = pl.ds(pl.multiple_of(j * tile, 128), tile)
            one = lax.dot_general(
                g[c, :, 0].reshape(total, uc), wg[cols, units_here], contract, preferred_element_type=F32
            )
            two = lax.dot_general(
                g[c, :, 1].reshape(total, uc), wu[cols, units_here], contract, preferred_element_type=F32
            )
            dx[:, cols] += one + two

    @pl.loop(0, s // tile)
    def _(j):
        cols = pl.ds(pl.multiple_of(j * tile, 128), tile)
        lined = jnp.dot(perm[1], dx[:, cols].astype(BF16), preferred_element_type=F32)
        dxp[:, :, :, cols] = lined.astype(BF16).reshape(2, nz, rows, tile)

    pair = remote(dxp.at[1 - core], pair_in, p_s, p_r, (d, sib))
    pair.start()
    for copy in peak_dp:
        copy.wait()
    peak = stats[...]
    for k in range(1, nd):
        peak = jnp.maximum(peak, st_dp[k - 1])
    stats[...] = peak
    peak_pair = remote(stats, st_pair, sp_s, sp_r, (d, sib))
    peak_pair.start()
    pair.wait_recv()
    line = []
    for k in range(1, nz):
        mixed = dxp[core, z_to[k]].astype(F32) + pair_in[z_to[k]].astype(F32)
        line_out[k - 1] = mixed.astype(BF16)
        copy = remote(line_out.at[k - 1], line_in.at[k - 1], l_s.at[k], l_r.at[k], (d, 2 * z_to[k] + core))
        copy.start()
        line.append(copy)
    peak_pair.wait()
    stats[...] = jnp.maximum(stats[...], st_pair[...])
    peak_line = [
        remote(stats, st_line.at[k - 1], sl_s.at[k], sl_r.at[k], (d, 2 * z_to[k] + core))
        for k in range(1, nz)
    ]
    for copy in peak_line:
        copy.start()
    reduced = dxp[core, z].astype(F32) + pair_in[z].astype(F32)
    for copy in line:
        copy.wait_recv()
    for k in range(1, nz):
        reduced = reduced + line_in[k - 1].astype(F32)
    wide[...] = reduced
    for i in range(nd):
        back[i] = wide[i * tl : (i + 1) * tl, :].astype(BF16)
    home = [
        remote(back.at[dp_to[k]], gtok.at[:, feature_cols(d)], o_s.at[k], o_r.at[k], (dp_to[k], t))
        for k in range(1, nd)
    ]
    for copy in home:
        copy.start()
    gtok[:, feature_cols(d)] = back[d]
    for copy in peak_line:
        copy.wait()
    peak = stats[...]
    for k in range(1, nz):
        peak = jnp.maximum(peak, st_line[k - 1])
    peaks[...] = peak
    for copy in sends + line + [pair]:
        copy.wait_send()

    @pl.loop(0, CHUNKS)
    def _(c):
        for k in range(1, nd):
            partial_copy(c, k).wait_send()
            grad_copy(c, k).wait_send()

    for copy in home:
        copy.wait()


def weight_grads(x, g, gate_out, up_out):
    chunks, nd, _, r, uc = g.shape
    contract = (((0,), (0,)), ((), ()))
    for side, out in ((0, gate_out), (1, up_out)):
        for c in range(chunks):
            out[:, c * uc : (c + 1) * uc] = lax.dot_general(
                x[...], g[c, :, side].reshape(nd * r, uc), contract, preferred_element_type=F32
            ).astype(BF16)


def orders(nd, nt, tl):
    total = nd * nt * tl
    index = np.arange(total).reshape(nd, nt, tl)
    arrived = np.arange(total).reshape(nt, nd, tl).transpose(1, 0, 2).reshape(-1)
    leaving = index.reshape(nd, nt // 2, 2, tl).transpose(2, 1, 0, 3).reshape(-1)
    eye = np.eye(total, dtype=np.float32)
    return jnp.asarray(np.stack([eye[arrived], eye[leaving]]), BF16)


def local(nd, nt, tokens, gate_weight, up_weight, cotangent):
    tl, _ = tokens.shape
    s, units = gate_weight.shape
    r = cotangent.shape[0]
    total = nd * r
    rows = nd * tl
    nz = nt // 2
    uc = units // CHUNKS
    dma = pltpu.SemaphoreType.DMA
    vmem = pl.BlockSpec(memory_space=pltpu.VMEM)
    hbm = pl.BlockSpec(memory_space=pl.ANY)
    weight_bytes = 2 * s * units * 2
    hidden, x, g, grad_tokens, peaks = pl.pallas_call(
        functools.partial(exchange, nd, nt),
        out_shape=(
            jax.ShapeDtypeStruct((r, units), BF16),
            jax.ShapeDtypeStruct((total, s), BF16),
            jax.ShapeDtypeStruct((CHUNKS, nd, 2, r, uc), BF16),
            jax.ShapeDtypeStruct((tl, nd * s), BF16),
            jax.ShapeDtypeStruct((2, 8, 128), F32),
        ),
        in_specs=[vmem, hbm, hbm, vmem, vmem],
        out_specs=(vmem,) * 5,
        scratch_shapes=[
            pltpu.VMEM((s, units), BF16),
            pltpu.VMEM((s, units), BF16),
            pltpu.VMEM((nd, tl, s), BF16),
            pltpu.VMEM((rows, s), F32),
            pltpu.VMEM((nt, rows, s), BF16),
            pltpu.VMEM((CHUNKS, nd, 2, r, uc), BF16),
            pltpu.VMEM((CHUNKS, nd - 1, 2, r, uc), BF16),
            pltpu.VMEM((total, s), F32),
            pltpu.VMEM((2, nz, rows, s), BF16),
            pltpu.VMEM((nz, rows, s), BF16),
            pltpu.VMEM((nz - 1, rows, s), BF16),
            pltpu.VMEM((nz - 1, rows, s), BF16),
            pltpu.VMEM((nd, tl, s), BF16),
            pltpu.VMEM((2, 8, 128), F32),
            pltpu.VMEM((nd - 1, 2, 8, 128), F32),
            pltpu.VMEM((2, 8, 128), F32),
            pltpu.VMEM((nz - 1, 2, 8, 128), F32),
            dma((2, CHUNKS)),
            dma((nd,)), dma((nd,)),
            dma((nz,)), dma((nz,)),
            dma((nz,)), dma((nz,)),
            dma, dma,
            dma((CHUNKS, nd)), dma((CHUNKS, nd)),
            dma((CHUNKS, nd)), dma((CHUNKS, nd)),
            dma((nz,)), dma((nz,)),
            dma((nd,)), dma((nd,)),
            dma((nd,)), dma((nd,)),
            dma, dma,
            dma((nz,)), dma((nz,)),
        ],
        compiler_params=pltpu.CompilerParams(
            collective_id=0, has_side_effects=True, vmem_limit_bytes=48 * 2**20
        ),
        cost_estimate=pl.CostEstimate(
            flops=8 * total * s * units, bytes_accessed=weight_bytes, transcendentals=r * units
        ),
    )(tokens, gate_weight, up_weight, cotangent, orders(nd, nt, tl))

    tile = min(256, s)
    grad_gate, grad_up = pl.pallas_call(
        weight_grads,
        grid=(s // tile,),
        out_shape=(jax.ShapeDtypeStruct((s, units), BF16),) * 2,
        in_specs=[
            pl.BlockSpec((total, tile), lambda i: (0, i)),
            pl.BlockSpec((CHUNKS, nd, 2, r, uc), lambda i: (0, 0, 0, 0, 0)),
        ],
        out_specs=(pl.BlockSpec((tile, units), lambda i: (i, 0)),) * 2,
        compiler_params=pltpu.CompilerParams(vmem_limit_bytes=32 * 2**20),
        cost_estimate=pl.CostEstimate(
            flops=4 * total * s * units, bytes_accessed=weight_bytes, transcendentals=0
        ),
    )(x, g)
    descales = (jnp.max(peaks, axis=(1, 2)) + EPSILON) / FP_MAX
    return (hidden, grad_tokens, grad_gate, grad_up, descales[0], descales[1])


def solution(mesh):
    nd = mesh.shape["dp"]
    nt = mesh.shape["tensor"]
    return jax.shard_map(
        functools.partial(local, nd, nt),
        mesh=mesh,
        in_specs=(
            P(("dp", "tensor"), None),
            P("dp", "tensor"),
            P("dp", "tensor"),
            P("dp", "tensor"),
        ),
        out_specs=(
            P("dp", "tensor"),
            P(("dp", "tensor"), None),
            P("dp", "tensor"),
            P("dp", "tensor"),
            P(),
            P(),
        ),
        check_vma=False,
    )
```

time: 458 us -> 70.7 us (0.15)
  other arithmetic: 169 us -> 0.11 us
  blocking collectives: 96.7 us -> 0 us
  Pallas kernels: 0 us -> 65.3 us
  matrix products: 57.8 us -> 0 us
  waiting for transfers between devices: 54 us -> 0 us
  local copies, waits for them, and re-layouts: 53.7 us -> 4.45 us
  between operations: 18.1 us -> 0.65 us
  starting transfers between devices: 7.41 us -> 0 us
    add x4 -> x0, other arithmetic: 101 us -> none  [add_replica(): return grad_total + settle(matrix_product * both_descale)]
    pmax x2 -> x0, blocking collectives: 81.7 us -> none  [the longest x1 42.2 us: local(): lax.pmax(jnp.max(jnp.abs(tokens)).astype(jnp.float32), ('dp', 'tensor'))]
    pallas_call x0 -> x2, Pallas kernels: none -> 65.3 us  [the longest x1 57.4 us: local(): pl.pallas_call(functools.partial(exchange, nd, nt), out_shape=(jax.ShapeD...]
    dot_general x6 -> x0, matrix products: 57.8 us -> none  [the longest x4 36.1 us: add_replica(): lax.dot_general(token_rows, grad_cols, contract, preferred_element_type=j...]
    unnamed x3 -> x0, other arithmetic: 46.1 us -> none
    reduce_scatter x1 -> x0, waiting for transfers between devices: 28.1 us -> none  [local(): lax.psum_scatter(jnp.dot(block_of_rows, weight_matrices, preferred_elemen...]
    all_gather x1 -> x0, waiting for transfers between devices: 25.9 us -> none  [local(): lax.all_gather(grad_quant.reshape(tokens_per_replica, 1, 2 * units), 'dp'...]
    another operation x1 -> x0, other arithmetic: 17.4 us -> none
  transfers between devices with their start and end apart: 5 -> 0, of which waited for: 2 -> 0; matrix products, arithmetic and copies ran while one was open for 40% -> 0% of each run, Pallas kernels for 0% -> 0%
where the time goes in v1:
time: 70.7 us; the launch traced here: 70.5 us
  Pallas kernels  65.3 us (92%)
  local copies, waits for them, and re-layouts  4.45 us (6%)
    pallas_call x1, Pallas kernels, local(): pl.pallas_call(functools.partial(exchange, nd, nt), out_shape=(jax.ShapeD...  57.4 us
    pallas_call x1, Pallas kernels, local(): pl.pallas_call(weight_grads, grid=(s // tile,), out_shape=(jax.ShapeDtype...  7.83 us
    unnamed x8, local copies, waits for them, and re-layouts  3.86 us

profile of v1, /device:TPU:0, one launch (start us, length us, event | category | flops | bytes accessed | tf_op | source)
XLA Modules:
  0.0 70.5 jit_solution(1302739795714682030)
XLA Ops:
  0.6 0.0 copy-start
  0.6 0.9 %copy-done = bf16[32,2048]{1,0:T(8,128)(2,1)S(1)} copy-done((bf16[32,2048]{1,0:T(8,128)(2,1)S(1)}, bf16[32,2048]{1,0:T(8,128)(2,1)}, u32[]{:S(2)}) %copy-start) | copy-done | bytes 131096
  1.5 0.0 copy-start.1
  1.5 0.8 %copy-done.1 = bf16[4,8192]{1,0:T(4,128)(2,1)S(1)} copy-done((bf16[4,8192]{1,0:T(4,128)(2,1)S(1)}, bf16[4,8192]{1,0:T(4,128)(2,1)}, u32[]{:S(2)}) %copy-start.1) | copy-done | bytes 65560
  2.4 0.0 copy-start.2
  2.4 0.8 %copy-done.2 = bf16[2,128,128]{2,1,0:T(8,128)(2,1)S(1)} copy-done((bf16[2,128,128]{2,1,0:T(8,128)(2,1)S(1)}, bf16[2,128,128]{2,1,0:T(8,128)(2,1)}, u32[]{:S(2)}) %copy-start.2) | copy-done | bytes 65560
  3.2 57.4 %shard_map.100 = (bf16[32,2048]{1,0:T(8,128)(2,1)S(1)}, bf16[128,2048]{1,0:T(8,128)(2,1)S(1)}, bf16[4,4,2,32,512]{4,3,2,1,0:T(8,128)(2,1)S(1)}, bf16[4,8192]{1,0:T(4,128)(2,1)S(1)}, f32[2,8,128]{2,1,0:T(8,128)S(1)}) custom-call(bf16[4,8192]{1,0:T(4,128)(2,1)S(1)} %copy-done.1, bf16[2048,2048]{1,0:T(8,128)(2,1)} %gate_hbm.1, bf16[2048,2048]{1,0:T(8,128)(2,1)} %up_hbm.1, ...), custom_call_target="tpu_custom_call" | custom-call | flops 4294967296 | bytes 16777216 | tf_op jit(solution)/shard_map/pallas_call | solution.py:284
  60.7 0.1 reduce_max.9
  60.8 0.6 fusion
  61.4 7.8 %shard_map.101 = (bf16[2048,2048]{1,0:T(8,128)(2,1)}, bf16[2048,2048]{1,0:T(8,128)(2,1)}) custom-call(bf16[128,2048]{1,0:T(8,128)(2,1)S(1)} %get-tuple-element.15.x, bf16[4,4,2,32,512]{4,3,2,1,0:T(8,128)(2,1)S(1)} %get-tuple-element.16.g), custom_call_target="tpu_custom_call" | custom-call | flops 2147483648 | bytes 16777216 | tf_op jit(solution)/shard_map/pallas_call | solution.py:335
  69.2 0.7 copy.13
  69.8 0.6 copy.14
  (1 shorter events, 0.0 us)
Async XLA Ops:
  0.6 0.9 %copy-start = (bf16[32,2048]{1,0:T(8,128)(2,1)S(1)}, bf16[32,2048]{1,0:T(8,128)(2,1)}, u32[]{:S(2)}) copy-start(bf16[32,2048]{1,0:T(8,128)(2,1)} %cot.1) | copy-start | bytes 393220
  1.5 0.8 %copy-start.1 = (bf16[4,8192]{1,0:T(4,128)(2,1)S(1)}, bf16[4,8192]{1,0:T(4,128)(2,1)}, u32[]{:S(2)}) copy-start(bf16[4,8192]{1,0:T(4,128)(2,1)} %tok.1) | copy-start | bytes 196612
  2.4 0.8 %copy-start.2 = (bf16[2,128,128]{2,1,0:T(8,128)(2,1)S(1)}, bf16[2,128,128]{2,1,0:T(8,128)(2,1)}, u32[]{:S(2)}) copy-start(bf16[2,128,128]{2,1,0:T(8,128)(2,1)} %constant.9.clone.perm) | copy-start | bytes 196612

commit v2 on v1

--- a/solution.py
+++ b/solution.py
@@ -2,7 +2,6 @@
 
 import jax
 import jax.numpy as jnp
-import numpy as np
 from jax import lax
 from jax.experimental import pallas as pl
 from jax.experimental.pallas import tpu as pltpu
@@ -33,9 +32,9 @@
 
 def exchange(
     nd, nt,
-    tok, gate_hbm, up_hbm, cot, perm,
+    tok, gate_hbm, up_hbm, cot,
     hid, x, g, gtok, peaks,
-    wg, wu, blocks, wide, xt, part, inbox, dx, dxp, pair_in, line_out, line_in, back,
+    perm, wg, wu, blocks, wide, xt, part, inbox, dx, dxp, pair_in, line_out, line_in, back,
     stats, st_dp, st_pair, st_line,
     w_sem, a_s, a_r, b_s, b_r, f_s, f_r, p_s, p_r, rs_s, rs_r, ag_s, ag_r,
     l_s, l_r, o_s, o_r, sd_s, sd_r, sp_s, sp_r, sl_s, sl_r,
@@ -64,10 +63,6 @@
             pltpu.make_async_copy(up_hbm.at[:, cols], wu.at[:, cols], w_sem.at[1, c]),
         )
 
-    for c in range(CHUNKS):
-        for copy in weight_copies(c):
-            copy.start()
-
     barrier = pltpu.get_barrier_semaphore()
     for k in range(1, nd):
         pl.semaphore_signal(barrier, inc=1, device_id=(dp_to[k], t), device_id_type=MESH)
@@ -85,6 +80,10 @@
         copy = remote(tok.at[:, feature_cols(dp_to[k])], blocks.at[d], a_s.at[k], a_r.at[k], (dp_to[k], t))
         copy.start()
         first.append(copy)
+    for c in range(CHUNKS):
+        for copy in weight_copies(c):
+            copy.start()
+
     blocks[d] = tok[:, feature_cols(d)]
     token_peak = lane_peak(jnp.abs(tok[...].astype(F32)), tl)
     stats[0] = jnp.broadcast_to(jnp.max(token_peak, axis=0, keepdims=True), (8, 128))
@@ -102,6 +101,15 @@
         copy.start()
     across = [remote(xt.at[t], xt.at[t], f_s.at[0], f_r.at[0], (d, sib))]
     across[0].start()
+    row = lax.broadcasted_iota(jnp.int32, (total, 1), 0)
+    col = lax.broadcasted_iota(jnp.int32, (total, total), 1)
+    inner = lax.rem(row, tl)
+    arrived = lax.rem(lax.div(row, tl), nt) * rows + lax.div(row, r) * tl + inner
+    end = lax.div(row, rows)
+    tensor_at = 2 * lax.rem(end, nz) + lax.div(end, nz)
+    leaving = lax.rem(lax.div(row, tl), nd) * r + tensor_at * tl + inner
+    for i, order in enumerate((arrived, leaving)):
+        perm[i] = jnp.where(col == order, 1.0, 0.0).astype(BF16)
     for k in range(1, nz):
         along[k - 1].wait_recv()
         slot = 2 * z_from[k] + core
@@ -258,15 +266,6 @@
             out[:, c * uc : (c + 1) * uc] = lax.dot_general(
                 x[...], g[c, :, side].reshape(nd * r, uc), contract, preferred_element_type=F32
             ).astype(BF16)
-
-
-def orders(nd, nt, tl):
-    total = nd * nt * tl
-    index = np.arange(total).reshape(nd, nt, tl)
-    arrived = np.arange(total).reshape(nt, nd, tl).transpose(1, 0, 2).reshape(-1)
-    leaving = index.reshape(nd, nt // 2, 2, tl).transpose(2, 1, 0, 3).reshape(-1)
-    eye = np.eye(total, dtype=np.float32)
-    return jnp.asarray(np.stack([eye[arrived], eye[leaving]]), BF16)
 
 
 def local(nd, nt, tokens, gate_weight, up_weight, cotangent):
@@ -290,9 +289,10 @@
             jax.ShapeDtypeStruct((tl, nd * s), BF16),
             jax.ShapeDtypeStruct((2, 8, 128), F32),
         ),
-        in_specs=[vmem, hbm, hbm, vmem, vmem],
+        in_specs=[vmem, hbm, hbm, vmem],
         out_specs=(vmem,) * 5,
         scratch_shapes=[
+            pltpu.VMEM((2, total, total), BF16),
             pltpu.VMEM((s, units), BF16),
             pltpu.VMEM((s, units), BF16),
             pltpu.VMEM((nd, tl, s), BF16),
@@ -329,9 +329,9 @@
         cost_estimate=pl.CostEstimate(
             flops=8 * total * s * units, bytes_accessed=weight_bytes, transcendentals=r * units
         ),
-    )(tokens, gate_weight, up_weight, cotangent, orders(nd, nt, tl))
-
-    tile = min(256, s)
+    )(tokens, gate_weight, up_weight, cotangent)
+
+    tile = min(512, s)
     grad_gate, grad_up = pl.pallas_call(
         weight_grads,
         grid=(s // tile,),

time: 70.7 us -> 69.3 us (0.980)
  local copies, waits for them, and re-layouts: 4.45 us -> 3.61 us
    unnamed x8 -> x6, local copies, waits for them, and re-layouts: 3.86 us -> 3.02 us
where the time goes in v2:
time: 69.3 us; the launch traced here: 69.1 us
  Pallas kernels  64.8 us (94%)
  local copies, waits for them, and re-layouts  3.61 us (5%)
    pallas_call x1, Pallas kernels, local(): pl.pallas_call(functools.partial(exchange, nd, nt), out_shape=(jax.ShapeD...  57.4 us
    pallas_call x1, Pallas kernels, local(): pl.pallas_call(weight_grads, grid=(s // tile,), out_shape=(jax.ShapeDtype...  7.33 us
    unnamed x6, local copies, waits for them, and re-layouts  3.02 us

profile of v2, /device:TPU:0, one launch (start us, length us, event | category | flops | bytes accessed | tf_op | source)
XLA Modules:
  0.0 69.1 jit_solution(1700325765870869933)
XLA Ops:
  0.6 0.0 copy-start
  0.6 0.9 %copy-done = bf16[32,2048]{1,0:T(8,128)(2,1)S(1)} copy-done((bf16[32,2048]{1,0:T(8,128)(2,1)S(1)}, bf16[32,2048]{1,0:T(8,128)(2,1)}, u32[]{:S(2)}) %copy-start) | copy-done | bytes 131096
  1.5 0.0 copy-start.1
  1.5 0.8 %copy-done.1 = bf16[4,8192]{1,0:T(4,128)(2,1)S(1)} copy-done((bf16[4,8192]{1,0:T(4,128)(2,1)S(1)}, bf16[4,8192]{1,0:T(4,128)(2,1)}, u32[]{:S(2)}) %copy-start.1) | copy-done | bytes 65560
  2.4 57.4 %shard_map.91 = (bf16[32,2048]{1,0:T(8,128)(2,1)S(1)}, bf16[128,2048]{1,0:T(8,128)(2,1)S(1)}, bf16[4,4,2,32,512]{4,3,2,1,0:T(8,128)(2,1)S(1)}, bf16[4,8192]{1,0:T(4,128)(2,1)S(1)}, f32[2,8,128]{2,1,0:T(8,128)S(1)}) custom-call(bf16[4,8192]{1,0:T(4,128)(2,1)S(1)} %copy-done.1, bf16[2048,2048]{1,0:T(8,128)(2,1)} %gate_hbm.1, bf16[2048,2048]{1,0:T(8,128)(2,1)} %up_hbm.1, ...), custom_call_target="tpu_custom_call" | custom-call | flops 4294967296 | bytes 16777216 | tf_op jit(solution)/shard_map/pallas_call | solution.py:283
  59.8 0.1 reduce_max.9
  59.9 0.6 fusion
  60.5 7.3 %shard_map.92 = (bf16[2048,2048]{1,0:T(8,128)(2,1)}, bf16[2048,2048]{1,0:T(8,128)(2,1)}) custom-call(bf16[128,2048]{1,0:T(8,128)(2,1)S(1)} %get-tuple-element.15.x, bf16[4,4,2,32,512]{4,3,2,1,0:T(8,128)(2,1)S(1)} %get-tuple-element.16.g), custom_call_target="tpu_custom_call" | custom-call | flops 2147483648 | bytes 16777216 | tf_op jit(solution)/shard_map/pallas_call | solution.py:335
  67.9 0.7 copy.12
  68.5 0.6 copy.13
  (1 shorter events, 0.0 us)
Async XLA Ops:
  0.6 0.9 %copy-start = (bf16[32,2048]{1,0:T(8,128)(2,1)S(1)}, bf16[32,2048]{1,0:T(8,128)(2,1)}, u32[]{:S(2)}) copy-start(bf16[32,2048]{1,0:T(8,128)(2,1)} %cot.1) | copy-start | bytes 393220
  1.5 0.8 %copy-start.1 = (bf16[4,8192]{1,0:T(4,128)(2,1)S(1)}, bf16[4,8192]{1,0:T(4,128)(2,1)}, u32[]{:S(2)}) copy-start(bf16[4,8192]{1,0:T(4,128)(2,1)} %tok.1) | copy-start | bytes 196612

commit v3 on v2

--- a/solution.py
+++ b/solution.py
@@ -51,7 +51,7 @@
     total = nd * r
     rows = nd * tl
     uc = units // CHUNKS
-    tile = min(256, s)
+    tile = min(512, s)
     dp_to = [lax.rem(d + k, nd) for k in range(nd)]
     z_to = [lax.rem(z + k, nz) for k in range(nz)]
     z_from = [lax.rem(z + nz - k, nz) for k in range(nz)]

time: 69.3 us -> 67.4 us (0.973)
  Pallas kernels: 64.8 us -> 62.9 us
    pallas_call x1, Pallas kernels: 57.4 us -> 55.6 us  [local(): pl.pallas_call(functools.partial(exchange, nd, nt), out_shape=(jax.ShapeD...]
where the time goes in v3:
time: 67.4 us; the launch traced here: 67.3 us
  Pallas kernels  62.9 us (93%)
  local copies, waits for them, and re-layouts  3.61 us (5%)
    pallas_call x1, Pallas kernels, local(): pl.pallas_call(functools.partial(exchange, nd, nt), out_shape=(jax.ShapeD...  55.6 us
    pallas_call x1, Pallas kernels, local(): pl.pallas_call(weight_grads, grid=(s // tile,), out_shape=(jax.ShapeDtype...  7.33 us
    unnamed x6, local copies, waits for them, and re-layouts  3.02 us

profile of v3, /device:TPU:0, one launch (start us, length us, event | category | flops | bytes accessed | tf_op | source)
XLA Modules:
  0.0 67.3 jit_solution(2811549525179345610)
XLA Ops:
  0.6 0.0 copy-start
  0.6 0.9 %copy-done = bf16[32,2048]{1,0:T(8,128)(2,1)S(1)} copy-done((bf16[32,2048]{1,0:T(8,128)(2,1)S(1)}, bf16[32,2048]{1,0:T(8,128)(2,1)}, u32[]{:S(2)}) %copy-start) | copy-done | bytes 131096
  1.5 0.0 copy-start.1
  1.5 0.8 %copy-done.1 = bf16[4,8192]{1,0:T(4,128)(2,1)S(1)} copy-done((bf16[4,8192]{1,0:T(4,128)(2,1)S(1)}, bf16[4,8192]{1,0:T(4,128)(2,1)}, u32[]{:S(2)}) %copy-start.1) | copy-done | bytes 65560
  2.4 55.6 %shard_map.91 = (bf16[32,2048]{1,0:T(8,128)(2,1)S(1)}, bf16[128,2048]{1,0:T(8,128)(2,1)S(1)}, bf16[4,4,2,32,512]{4,3,2,1,0:T(8,128)(2,1)S(1)}, bf16[4,8192]{1,0:T(4,128)(2,1)S(1)}, f32[2,8,128]{2,1,0:T(8,128)S(1)}) custom-call(bf16[4,8192]{1,0:T(4,128)(2,1)S(1)} %copy-done.1, bf16[2048,2048]{1,0:T(8,128)(2,1)} %gate_hbm.1, bf16[2048,2048]{1,0:T(8,128)(2,1)} %up_hbm.1, ...), custom_call_target="tpu_custom_call" | custom-call | flops 4294967296 | bytes 16777216 | tf_op jit(solution)/shard_map/pallas_call | solution.py:283
  58.0 0.1 reduce_max.9
  58.1 0.6 fusion
  58.6 7.3 %shard_map.92 = (bf16[2048,2048]{1,0:T(8,128)(2,1)}, bf16[2048,2048]{1,0:T(8,128)(2,1)}) custom-call(bf16[128,2048]{1,0:T(8,128)(2,1)S(1)} %get-tuple-element.15.x, bf16[4,4,2,32,512]{4,3,2,1,0:T(8,128)(2,1)S(1)} %get-tuple-element.16.g), custom_call_target="tpu_custom_call" | custom-call | flops 2147483648 | bytes 16777216 | tf_op jit(solution)/shard_map/pallas_call | solution.py:335
  66.0 0.7 copy.12
  66.6 0.6 copy.13
  (1 shorter events, 0.0 us)
Async XLA Ops:
  0.6 0.9 %copy-start = (bf16[32,2048]{1,0:T(8,128)(2,1)S(1)}, bf16[32,2048]{1,0:T(8,128)(2,1)}, u32[]{:S(2)}) copy-start(bf16[32,2048]{1,0:T(8,128)(2,1)} %cot.1) | copy-start | bytes 393220
  1.5 0.8 %copy-start.1 = (bf16[4,8192]{1,0:T(4,128)(2,1)S(1)}, bf16[4,8192]{1,0:T(4,128)(2,1)}, u32[]{:S(2)}) copy-start(bf16[4,8192]{1,0:T(4,128)(2,1)} %tok.1) | copy-start | bytes 196612
